TPU v7x, 512 devices: a whole 4x8x8 slice. The times are simulated.
512 devices in a mesh: gx: 32 (over z, x), gy: 16 (over y, core).
Axes of the slice: x: 4, y: 8, z: 8, core: 2. Of those that a mesh axis runs over, the one named last changes fastest.
Arguments:
- prior_basis: float32 [512, 512, 128], P('gx', 'gy'), may hold values from -6 to 6
- cond_x: float32 [512, 512], P('gx', 'gy'), may hold values from 0.5 to 5
- cond_y: float32 [512, 512], P('gx', 'gy'), may hold values from 0.5 to 5
- capacitance: float32 [512, 512], P('gx', 'gy'), may hold values from 0.05 to 1
- pad_mask: int32 [512, 512], P('gx', 'gy'), may hold values 0 or 1
- port_nodes: int32 [128], replicated, may hold values from 0 to 262143
Outputs:
- new_basis: float32 [512, 512, 128], P('gx', 'gy')
- reduced_g: float32 [128, 128], replicated
- reduced_c: float32 [128, 128], replicated
Inputs may be any that keep to these rules, and one draw needn't show every extreme that they name: `port_nodes`: a row-major node index into the grid of 512 x 512 nodes.
All inputs are finite; a program needn't handle non-finite values. No bound on the sum of `pad_mask` on one device may be relied on, other than what follows from the above.
Results may differ from a plain program's by a relative error of at most 0.0003.
Values sent between devices are 32-bit elements; how exact they have to be, the bound alone decides.
A program may use at most 64 MiB of HBM per device.

v0:
```python
import jax
import jax.numpy as jnp
from jax import lax
from jax.sharding import PartitionSpec as P

SWEEPS = 4


shift_point = 0.5
supply_conductance = 4.0
port_current = 8.0
highest = lax.Precision.HIGHEST


def shifted(shard, axis, by):
    devices = lax.axis_size(axis)
    pairs = [(i, i + by) for i in range(devices) if 0 <= i + by < devices]
    return lax.ppermute(shard, axis, pairs)


def padded(cells, sides, width):
    for axis, dim in sides:
        count = lax.axis_size(axis)
        ends = count - 1
        head = lax.slice_in_dim(cells, 0, width, axis=dim)
        tail = lax.slice_in_dim(cells, cells.shape[dim] - width, cells.shape[dim], axis=dim)
        cells = jnp.concatenate(
            [
                lax.ppermute(tail, axis, [(i, (i + 1) % count) for i in range(ends)]),
                cells,
                lax.ppermute(head, axis, [((i + 1) % count, i) for i in range(ends)]),
            ],
            axis=dim,
        )
    return cells


def neighbors(ext, links):
    cx, cy, cx_up, cy_left = links
    total = cx[:, :, None] * ext[2:, 1:-1] + cx_up[:, :, None] * ext[:-2, 1:-1]
    return total + cy[:, :, None] * ext[1:-1, 2:] + cy_left[:, :, None] * ext[1:-1, :-2]


def local_inner(left, right):
    a = left.reshape(-1, left.shape[-1])
    b = right.reshape(-1, right.shape[-1])
    return jnp.einsum("cp,cq->pq", a, b, precision=highest, preferred_element_type=jnp.float32)


def per_device(prior_basis, cond_x, cond_y, capacitance, pad_mask, port_nodes):
    rows_dev, cols_dev = cond_x.shape
    width = port_nodes.shape[0]
    count_x = lax.axis_size("gx")
    count_y = lax.axis_size("gy")
    total_rows = rows_dev * count_x
    total_cols = cols_dev * count_y
    nodes = total_rows * total_cols
    row_start = lax.axis_index("gx") * rows_dev
    col_start = lax.axis_index("gy") * cols_dev
    global_rows = row_start + jnp.arange(rows_dev, dtype=jnp.int32)[:, None]
    global_cols = col_start + jnp.arange(cols_dev, dtype=jnp.int32)[None, :]
    cx = jnp.where(global_rows < total_rows - 1, cond_x, jnp.float32(0.0))
    cy = jnp.where(global_cols < total_cols - 1, cond_y, jnp.float32(0.0))
    above = shifted(cx[-1:, :], "gx", 1)
    beside = shifted(cy[:, -1:], "gy", 1)
    cx_up = jnp.concatenate([above, cx[:-1]], axis=0)
    cy_left = jnp.concatenate([beside, cy[:, :-1]], axis=1)
    links = (cx, cy, cx_up, cy_left)
    diag_g = cx + cx_up + cy + cy_left + supply_conductance * pad_mask.astype(jnp.float32)
    diag = (diag_g + shift_point * capacitance)[:, :, None]
    node_ids = global_rows * total_cols + global_cols
    onehot = (node_ids[:, :, None] == port_nodes[None, None, :]).astype(jnp.float32)
    rhs = capacitance[:, :, None] * prior_basis + port_current * onehot

    def sweep(step, current):
        ext = padded(current, (("gx", 0), ("gy", 1)), 1)
        return (rhs + neighbors(ext, links)) / diag

    field = lax.fori_loop(0, SWEEPS, sweep, rhs / diag)
    proj = lax.psum(local_inner(prior_basis, field), ("gx", "gy")) / nodes
    cand = field - jnp.einsum("xyk,kp->xyp", prior_basis, proj, precision=highest)
    gram = lax.psum(local_inner(cand, cand), ("gx", "gy")) / nodes
    lower = jnp.linalg.cholesky(gram)
    flat = cand.reshape(-1, width)
    basis_flat = lax.linalg.triangular_solve(
        lower, flat, left_side=False, lower=True, transpose_a=True
    )
    new_basis = basis_flat.reshape(rows_dev, cols_dev, width)
    ext = padded(new_basis, (("gx", 0), ("gy", 1)), 1)
    g_image = diag_g[:, :, None] * new_basis - neighbors(ext, links)
    g_raw, c_raw = lax.psum(
        (
            local_inner(new_basis, g_image),
            local_inner(new_basis, capacitance[:, :, None] * new_basis),
        ),
        ("gx", "gy"),
    )
    reduced_g = g_raw / nodes
    reduced_c = c_raw / nodes
    return (new_basis, reduced_g, reduced_c)


def solution(mesh):
    placed = (P("gx", "gy", None), P("gx", "gy"), P("gx", "gy"), P("gx", "gy"), P("gx", "gy"), P())
    return jax.shard_map(
        per_device,
        mesh=mesh,
        in_specs=placed,
        out_specs=(P("gx", "gy", None), P(), P()),
        check_vma=False,
    )
```

profile of v0, /device:TPU:1, one launch (start us, length us, event | category | flops | bytes accessed | tf_op | source)
XLA Modules:
  0.0 933.4 jit_solution(7570610463558537196)
XLA Ops:
  7.2 0.6 copy-done.5
  7.9 0.1 slice.102
  7.9 4.7 collective-permute-start.5
  12.7 0.1 broadcast_select_fusion.1
  12.8 3.1 collective-permute-start.4
  16.0 0.9 collective-permute-done.5
  16.9 0.1 multiply_add_fusion
  17.0 0.7 copy-done.7
  17.6 1.2 broadcast_divide_fusion
  18.9 72.1 %while.10 = (s32[]{:T(128)}, f32[16,32,128]{2,1,0:T(8,128)S(1)}, f32[16,32]{1,0:T(8,128)S(1)}, f32[16,32]{1,0:T(8,128)S(1)}, f32[16,32]{1,0:T(8,128)S(1)}, /*ind...) while((s32[]{:T(128)}, f32[16,32,128]{2,1,0:T(8,128)S(1)}, ...), condition=%wide.region_1.2_spmd, body=%wide.region_0.1_spmd.sunk | while | flops 851970 | bytes 2564349 | solution.py:79
  18.9 3.4 collective-permute-start
  22.3 1.3 collective-permute-start.1
  23.7 3.1 collective-permute-done.1
  26.8 4.5 collective-permute-start.2
  31.3 2.7 collective-permute-start.3
  34.1 2.2 collective-permute-done.3
  36.3 0.4 fusion.48
  36.8 3.1 collective-permute-start
  39.9 1.3 collective-permute-start.1
  41.3 5.0 collective-permute-done.1
  46.3 3.1 collective-permute-start.2
  49.4 1.9 collective-permute-start.3
  51.3 3.0 collective-permute-done.3
  54.4 0.4 fusion.48
  54.8 5.7 collective-permute-start
  60.6 1.3 collective-permute-start.1
  61.9 3.4 collective-permute-done.1
  65.4 3.1 collective-permute-start.2
  68.5 1.9 collective-permute-start.3
  70.4 3.0 collective-permute-done.3
  73.5 0.4 fusion.48
  73.9 3.7 collective-permute-start
  77.7 1.3 collective-permute-start.1
  79.0 3.4 collective-permute-done.1
  82.5 3.1 collective-permute-start.2
  85.6 1.9 collective-permute-start.3
  87.5 3.0 collective-permute-done.3
  90.6 0.4 fusion.48
  91.0 1.2 convolution_bitcast_fusion.2
  92.3 273.4 %all-reduce.5.cloned.1.call-done = f32[128,128]{0,1:T(8,128)} async-done(((f32[128,128]{0,1:T(8,128)}), f32[128,128]{0,1:T(8,128)}) %all-reduce.5.cloned.1.call-update) | async-done | bytes 65552 | tf_op jit(solution)/shard_map/psum | solution.py:80
  365.7 1.2 fusion.9
  366.9 1.2 convolution_bitcast_fusion.1
  368.2 255.1 %all-reduce.7.cloned.1.call-done = f32[128,128]{0,1:T(8,128)} async-done(((f32[128,128]{0,1:T(8,128)}), f32[128,128]{0,1:T(8,128)}) %all-reduce.7.cloned.1.call-update) | async-done | bytes 65552 | tf_op jit(solution)/shard_map/psum | solution.py:82
  623.3 0.8 broadcast_multiply_fusion.2
  624.2 0.1 copy.11
  624.3 0.7 copy-done.2
  625.0 11.7 %cholesky.16 = f32[128,128]{1,0:T(8,128)S(1)} custom-call(f32[128,128]{1,0:T(8,128)S(1)} %fusion.24), custom_call_target="Cholesky" | custom-call | tf_op jit(solution)/shard_map/jit(cholesky)/cholesky | solution.py:83
  636.8 0.6 compare_reduce_fusion
  637.4 0.7 fusion.21
  638.1 9.8 %custom-call.6 = f32[1,128,128]{1,2,0:T(8,128)S(1)} custom-call(f32[1,128,128]{2,1,0:T(8,128)S(1)} %fusion.21), custom_call_target="InvertDiagBlocksLowerTriangular" | custom-call | tf_op jit(solution)/shard_map/triangular_solve | solution.py:85
  647.9 0.4 fusion.22
  648.3 1.3 collective-permute-start.6
  649.6 4.0 collective-permute-start.7
  653.6 0.1 mul.144
  653.7 0.8 collective-permute-done.7
  654.5 1.9 collective-permute-start.8
  656.4 4.5 collective-permute-start.9
  660.9 1.3 fusion.10
  662.2 0.4 fusion.14
  662.6 1.2 fusion.33
  663.9 260.7 %all-reduce.9.cloned.1.call-done = (f32[128,128]{0,1:T(8,128)}, f32[128,128]{0,1:T(8,128)}) async-done(((f32[128,128]{0,1:T(8,128)}, f32[128,128]{0,1:T(8,128)}), (f32[128,128]{0,1:T(8,128)}, f32[128,128]{0,1:T(8,128)})) %all-reduce.9.cloned.1.call-update) | async-done | bytes 131088 | tf_op jit(solution)/shard_map/psum | solution.py:91
  924.5 0.9 broadcast_multiply_fusion
  925.4 0.7 copy.14
  926.1 0.7 copy.15
  (66 shorter events, 0.7 us)
Async XLA Ops:
  7.2 0.7 copy-start.5
  7.2 358.5 %all-reduce.5.cloned.1.call-start = ((), (), s32[]{:S(2)}) async-start(), calls=%async_computation | async-start | bytes 131072 | tf_op jit(solution)/shard_map/psum | solution.py:80
  7.9 4.7 copy-start.4
  7.9 8.9 collective-permute-start.5
  12.8 4.1 collective-permute-start.4
  15.9 1.0 copy-start.3
  15.9 1.0 copy-start.6
  17.0 0.7 copy-start.7
  18.9 72.1 %copy-start.1 = (f32[16,32,128]{2,1,0:T(8,128)S(1)}, f32[16,32,128]{2,1,0:T(8,128)}, u32[]{:S(2)}) copy-start(f32[16,32,128]{2,1,0:T(8,128)} %param.8) | copy-start | bytes 786436
  18.9 4.7 collective-permute-start
  22.3 4.5 collective-permute-start.1
  26.8 7.3 collective-permute-start.2
  31.3 5.0 collective-permute-start.3
  36.8 4.4 collective-permute-start
  39.9 6.3 collective-permute-start.1
  46.3 5.0 collective-permute-start.2
  49.4 5.0 collective-permute-start.3
  54.8 7.1 collective-permute-start
  60.6 4.8 collective-permute-start.1
  65.4 5.0 collective-permute-start.2
  68.5 5.0 collective-permute-start.3
  73.9 5.1 collective-permute-start
  77.7 4.8 collective-permute-start.1
  82.5 5.0 collective-permute-start.2
  85.6 5.0 collective-permute-start.3
  92.3 531.1 %all-reduce.7.cloned.1.call-start = ((), (), s32[]{:S(2)}) async-start(), calls=%async_computation.1 | async-start | bytes 131072 | tf_op jit(solution)/shard_map/psum | solution.py:82
  368.1 556.4 %all-reduce.9.cloned.1.call-start = ((), (), s32[]{:S(2)}) async-start(), calls=%async_computation.2 | async-start | bytes 262144 | tf_op jit(solution)/shard_map/psum | solution.py:91
  624.2 0.8 copy-start.2
  648.3 14.3 %copy-start = (f32[512,128]{1,0:T(8,128)}, f32[512,128]{1,0:T(8,128)S(1)}, u32[]{:S(2)}) copy-start(f32[512,128]{1,0:T(8,128)S(1)} %fusion.22) | copy-start | bytes 786436
  648.3 5.4 collective-permute-start.6
  649.6 4.8 collective-permute-start.7
  654.5 7.7 collective-permute-start.8
  656.4 5.8 collective-permute-start.9
Sparse Core Ops, SparseCore 0:
  92.4 273.2 all-reduce.4
  372.0 251.2 all-reduce.6
  664.0 260.5 all-reduce.8
where the time goes:
time: 934 us; the launch traced here: 933 us
  waiting for transfers between devices  817 us (87%)
  starting transfers between devices  63.1 us (7%)
  other arithmetic  28.1 us (3%)
  between operations  14 us (1%)
    psum x1, waiting for transfers between devices, per_device(): proj = lax.psum(local_inner(prior_basis, field), ('gx', 'gy')) / nodes  273 us
    psum x1, waiting for transfers between devices, per_device(): lax.psum((local_inner(new_basis, g_image), local_inner(new_basis, capacit...  261 us
    psum x1, waiting for transfers between devices, per_device(): gram = lax.psum(local_inner(cand, cand), ('gx', 'gy')) / nodes  255 us
    ppermute x10, starting transfers between devices, padded(): lax.ppermute(tail, axis, [(i, (i + 1) % count) for i in range(ends)])  38.2 us
    ppermute x10, waiting for transfers between devices, padded(): lax.ppermute(head, axis, [((i + 1) % count, i) for i in range(ends)])  26.3 us
  transfers between devices with their start and end apart: 25, of which 13 were waited for; matrix products, arithmetic and copies ran while one was open for 0% of the time, Pallas kernels for 0%

commit v1 on v0

v1 whole, which is shorter than its diff:
```python
import functools
import math

import jax
import jax.numpy as jnp
from jax import lax
from jax.experimental import pallas as pl
from jax.experimental.pallas import tpu as pltpu
from jax.sharding import PartitionSpec as P

SWEEPS = 4
SHIFT = 0.5
SUPPLY = 4.0
PORT = 8.0
MESH = pl.DeviceIdType.MESH
F32 = jnp.float32
UP, DOWN = SWEEPS, SWEEPS + 1
SIDE = 8
PAD = 8


def mm(a, b, ca, cb):
    return lax.dot_general(
        a, b, (((ca,), (cb,)), ((), ())), precision=lax.Precision.HIGHEST, preferred_element_type=F32
    )


def tn(a, b):
    return mm(a, b, 0, 0)


def nt(a, b):
    return mm(a, b, 1, 1)


def nn(a, b):
    return mm(a, b, 1, 0)


def inverse_factor(matrix):
    n = matrix.shape[0]
    tiles = [matrix[8 * t : 8 * t + 8] for t in range(n // 8)]
    lane = lax.broadcasted_iota(jnp.int32, (8, n), 1)
    sub = lax.broadcasted_iota(jnp.int32, (8, n), 0)

    def row(x, j):
        return jnp.broadcast_to(x[j : j + 1], x.shape)

    def column(x, k):
        return jnp.broadcast_to(x[:, k : k + 1], x.shape)

    rows = []
    for p in range(n // 8):
        g = tiles[p]
        cols = [column(g, 8 * p + j) for j in range(8)]
        kept = jnp.zeros((8, n), F32)
        for j in range(8):
            at = lane == 8 * p + j
            here = sub == j
            rj = row(g, j)
            pivot = row(cols[j], j)
            inv = 1.0 / pivot
            kept = jnp.where(here, jnp.where(at, 1.0, rj) * lax.rsqrt(pivot), kept)
            m = jnp.where(here, -inv, cols[j] * inv)
            for l in range(j + 1, 8):
                cols[l] = jnp.where(here, 0.0, cols[l]) - m * row(cols[l], j)
            g = jnp.where(at, -m, jnp.where(here, 0.0, g) - m * rj)
        rows.append(jnp.where(lane <= sub + 8 * p, kept, 0.0))
        if p + 1 < n // 8:
            w = [row(g, j) for j in range(8)]
            inside = (lane >= 8 * p) & (lane < 8 * p + 8)
            for t in range(p + 1, n // 8):
                x = jnp.where(inside, 0.0, tiles[t])
                for j in range(8):
                    x = x - column(tiles[t], 8 * p + j) * w[j]
                tiles[t] = x
    return rows


def reach(
    ngx, ngy, rows, cols,
    v_hbm, condx_hbm, condy_hbm, cap_hbm, pad_hbm, port_hbm,
    field_out, small_out,
    t0, t1, t2, t3, port, stack, q, qx, vx, cxs, cys, dis, caps, rhs, fa, fb, dgs,
    a0, a1, a2, r10, r11, r12, d0, d1, d2, r20, r21, r22, o0, o1, o2,
    lsem, vsend, vrecv, qsend, qrecv, s1, v1, s2, v2, s3, v3,
):
    gx, gy = lax.axis_index("gx"), lax.axis_index("gy")
    width = 128
    ext = rows + UP + DOWN
    wide = cols + 2 * SIDE
    nx, ny = ngx * rows, ngy * cols
    nodes = nx * ny

    loads = [
        pltpu.make_async_copy(s, d, lsem.at[k])
        for k, (s, d) in enumerate(
            ((condx_hbm, t0), (condy_hbm, t1), (cap_hbm, t2), (pad_hbm, t3), (port_hbm, port),
             (v_hbm, vx.at[pl.ds(UP, rows), pl.ds(SIDE, cols)]))
        )
    ]
    for copy in loads:
        copy.start()

    barrier = pltpu.get_barrier_semaphore()
    around = [(dx, dy) for dx in (-1, 0, 1) for dy in (-1, 0, 1) if dx or dy]

    def beside(dx, dy):
        return lax.rem(gx + ngx + dx, ngx), lax.rem(gy + ngy + dy, ngy)

    for dx, dy in around:
        if dx and dy:
            pl.semaphore_signal(barrier, inc=1, device_id=beside(dx, dy), device_id_type=MESH)

    def others(me, n, f):
        def step(k, c):
            f(lax.rem(me + k, n))
            return c

        lax.fori_loop(1, n, step, 0)

    others(gx, ngx, lambda p: pl.semaphore_signal(barrier, inc=1, device_id=(p, gy), device_id_type=MESH))
    others(gy, ngy, lambda p: pl.semaphore_signal(barrier, inc=1, device_id=(gx, p), device_id_type=MESH))

    stack[...] = jnp.zeros_like(stack)
    for copy in loads[:5]:
        copy.wait()
    for f, ref in enumerate((t0, t1, t2)):
        stack[f * rows : (f + 1) * rows, 0:cols] = ref[...]
    stack[3 * rows : 4 * rows, 0:cols] = t3[...].astype(F32)
    q[...] = stack[...].T[0:cols]
    pl.semaphore_wait(barrier, 4 + ngx - 1 + ngy - 1)

    sent = []
    for k, (dx, dy) in enumerate(around):
        to = beside(dx, dy)
        src_r, dst_r, n_r = ((0, UP + rows, DOWN), (0, UP, rows), (rows - UP, 0, UP))[dx + 1]
        src_c, dst_c, n_c = ((0, SIDE + cols, SIDE), (0, SIDE, cols), (cols - SIDE, 0, SIDE))[dy + 1]
        copy = pltpu.make_async_remote_copy(
            v_hbm.at[pl.ds(src_r, n_r), pl.ds(src_c, n_c)],
            vx.at[pl.ds(dst_r, n_r), pl.ds(dst_c, n_c)],
            vsend.at[k], vrecv.at[k], device_id=to, device_id_type=MESH,
        )
        copy.start()
        sent.append(copy)
        copy = pltpu.make_async_remote_copy(
            q.at[pl.ds(src_c, n_c)],
            qx.at[1 - dx, pl.ds(dst_c, n_c)],
            qsend.at[k], qrecv.at[k], device_id=to, device_id_type=MESH,
        )
        copy.start()
        sent.append(copy)

    def scatter(src, landed, send, recv):
        pc = landed.shape[1]

        def one(p):
            pltpu.make_async_remote_copy(
                src.at[pl.ds(pl.multiple_of(p * pc, 8), pc)], landed.at[gx], send, recv,
                device_id=(p, gy), device_id_type=MESH,
            ).start()

        others(gx, ngx, one)
        landed[gx] = src[pl.ds(pl.multiple_of(gx * pc, 8), pc)]

    def wait(landed, n, sem):
        part = landed.at[pl.ds(0, n - 1)]
        pltpu.make_async_copy(part, part, sem).wait()

    def total(landed):
        x = landed[0]
        for k in range(1, landed.shape[0]):
            x = x + landed[k]
        return x

    def exchange(part, landed, send, recv):
        def one(p):
            pltpu.make_async_remote_copy(
                part, landed.at[gy], send, recv, device_id=(gx, p), device_id_type=MESH
            ).start()

        others(gy, ngy, one)
        landed[gy] = part[...]

    def gather(value, whole, send, recv):
        pc = whole.shape[1]
        whole[gx] = value

        def one(p):
            pltpu.make_async_remote_copy(
                whole.at[gx], whole.at[gx], send, recv, device_id=(p, gy), device_id_type=MESH
            ).start()

        others(gx, ngx, one)

    sets = ((a0, r10, d0, r20, o0), (a1, r11, d1, r21, o1), (a2, r12, d2, r22, o2))

    def first(k):
        scatter(sets[k][0], sets[k][1], s1.at[k], v1.at[k])

    def second(k):
        wait(sets[k][1], ngx, v1.at[k])
        sets[k][2][...] = total(sets[k][1])
        exchange(sets[k][2], sets[k][3], s2.at[k], v2.at[k])

    def third(k):
        wait(sets[k][3], ngy, v2.at[k])
        gather(total(sets[k][3]), sets[k][4], s3.at[k], v3.at[k])

    def last(k):
        wait(sets[k][4], ngx, v3.at[k])

    def block(k, b):
        whole = sets[k][4]
        pc = whole.shape[1]
        per = width // pc if pc <= width else 0
        if per and width % pc == 0:
            return whole[b * per : (b + 1) * per].reshape(width, width)
        return whole[...].reshape(-1, width)[b * width : (b + 1) * width]

    qx[1, SIDE : SIDE + cols] = q[...]
    loads[5].wait()
    own_r, own_c = slice(UP, UP + rows), slice(SIDE, SIDE + cols)
    for i in range(rows):
        k = 2 * rows + i
        caps[UP + i, own_c] = jnp.broadcast_to(q[:, k : k + 1], (cols, width))
    v = vx[own_r, own_c].reshape(rows * cols, width)
    c_own = caps[own_r, own_c].reshape(rows * cols, width)
    a0[0:width] = tn(v, v)
    a0[width : 2 * width] = tn(v, c_own * v)
    first(0)
    for buf in (fa, fb, cys):
        buf[:, 0:PAD] = jnp.zeros((buf.shape[0], PAD, width), F32)
        buf[:, PAD + wide :] = jnp.zeros((buf.shape[0], PAD, width), F32)

    for copy in sent[1::2]:
        copy.wait_recv()
    lane = lax.broadcasted_iota(jnp.int32, (wide, width), 1)
    line = lax.broadcasted_iota(jnp.int32, (wide, width), 0)

    def whole_field(f):
        def at(x, first_row, lane_at):
            return pltpu.roll(x, (lane_at - (f * rows + first_row)) % width, 1)

        above = at(qx[0], rows - UP - 1, 0)
        own = at(qx[1], 0, UP + 1)
        below = at(qx[2], 0, UP + 1 + rows)
        return jnp.where(lane < UP + 1, above, jnp.where(lane < UP + 1 + rows, own, below))

    grow = lax.rem(gx * rows - UP - 1 + lane + nx, nx)
    gcol = lax.rem(gy * cols - SIDE + line + ny, ny)
    cx = jnp.where(grow == nx - 1, 0.0, whole_field(0))
    cy = jnp.where(gcol == ny - 1, 0.0, whole_field(1))
    cp = whole_field(2)
    dg = cx + pltpu.roll(cx, 1, 1) + cy + pltpu.roll(cy, 1, 0) + SUPPLY * whole_field(3)
    di = 1.0 / jnp.where((lane > 0) & (lane <= ext), dg + SHIFT * cp, 1.0)

    def spread(x, i):
        return jnp.broadcast_to(x[:, i + 1 : i + 2], (wide, width))

    cxs[0] = spread(cx, -1)
    for i in range(ext):
        cxs[i + 1] = spread(cx, i)
        cys[i, PAD : PAD + wide] = spread(cy, i)
        dis[i] = spread(di, i)
        caps[i] = spread(cp, i)
    for i in range(rows):
        dgs[i] = jnp.broadcast_to(dg[own_c, UP + i + 1 : UP + i + 2], (cols, width))

    for copy in sent[0::2]:
        copy.wait_recv()
    mid = slice(PAD, PAD + wide)
    rid = lax.rem(gy * cols - SIDE + line + ny, ny)

    def start(i, c):
        node = lax.rem(gx * rows - UP + i + nx, nx) * ny + rid
        r = caps[i] * vx[i] + jnp.where(node == port[...], PORT, 0.0)
        rhs[i] = r
        fa[i, mid] = r * dis[i]
        return c

    lax.fori_loop(0, ext, start, 0)

    src, dst = fa, fb
    for s in range(SWEEPS):
        def sweep(i, c, src=src, dst=dst):
            near = cxs[i + 1] * src[i + 1, mid] + cxs[i] * src[i - 1, mid]
            near = near + cys[i, mid] * src[i, PAD + 1 : PAD + 1 + wide]
            near = near + cys[i, PAD - 1 : PAD - 1 + wide] * src[i, PAD - 1 : PAD - 1 + wide]
            dst[i, mid] = (rhs[i] + near) * dis[i]
            return c

        lax.fori_loop(1 + s, ext - 1 - s, sweep, 0)
        src, dst = dst, src
        if s == 1:
            second(0)

    own_f = slice(PAD + SIDE, PAD + SIDE + cols)
    f = src[own_r, own_f].reshape(rows * cols, width)
    a1[0:width] = tn(v, f)
    a1[width : 2 * width] = tn(f, f)
    first(1)
    third(0)
    field_out[...] = f

    cxo = cxs[UP + 1 : UP + 1 + rows, own_c].reshape(rows * cols, width)
    cyo = cys[own_r, own_f].reshape(rows * cols, width)
    v_below = vx[UP + 1 : UP + 1 + rows, own_c].reshape(rows * cols, width)
    v_right = vx[own_r, SIDE + 1 : SIDE + 1 + cols].reshape(rows * cols, width)
    f_below = src[UP + 1 : UP + 1 + rows, own_f].reshape(rows * cols, width)
    f_right = src[own_r, PAD + SIDE + 1 : PAD + SIDE + 1 + cols].reshape(rows * cols, width)
    dgo = dgs[...].reshape(rows * cols, width)
    uv = cxo * v_below + cyo * v_right
    uf = cxo * f_below + cyo * f_right
    gv = dgo * v - uv
    a2[0:width] = tn(v, gv) - tn(uv, v)
    a2[width : 2 * width] = tn(gv, f) - tn(v, uf)
    a2[2 * width : 3 * width] = tn(f, dgo * f - uf) - tn(uf, f)
    cf = c_own * f
    a2[3 * width : 4 * width] = tn(v, cf)
    a2[4 * width : 5 * width] = tn(f, cf)
    a2[5 * width :] = jnp.zeros((a2.shape[0] - 5 * width, width), F32)
    second(1)
    first(2)
    third(1)
    second(2)
    last(0)
    last(1)

    vv, vcv = block(0, 0) / nodes, block(0, 1) / nodes
    proj, ff = block(1, 0) / nodes, block(1, 1) / nodes
    z = nn(vv, proj) - 2.0 * proj
    gram = ff + tn(proj, z)
    third(2)
    for t, r in enumerate(inverse_factor(gram)):
        small_out[8 * t : 8 * t + 8] = r
    small_out[width : 2 * width] = proj
    last(2)
    vgv, vgf, fgf = (block(2, b) / nodes for b in range(3))
    vcf, fcf = (block(2, b) / nodes for b in range(3, 5))
    small_out[2 * width : 3 * width] = fgf - tn(vgf, proj) + tn(proj, nn(vgv, proj) - vgf)
    small_out[3 * width : 4 * width] = fcf - tn(vcf, proj) + tn(proj, nn(vcv, proj) - vcf)

    for copy in sent:
        copy.wait_send()
    for k in range(3):
        wait(sets[k][1], ngx, s1.at[k])
        wait(sets[k][3], ngy, s2.at[k])
        wait(sets[k][4], ngx, s3.at[k])


def finish(v_ref, f_ref, small_ref, basis_ref, g_ref, c_ref):
    w = 128
    linv = small_ref[0:w]
    y = nt(linv, small_ref[w : 2 * w])
    basis_ref[...] = nt(f_ref[...], linv) - nt(v_ref[...], y)
    g_ref[...] = nt(nn(linv, small_ref[2 * w : 3 * w]), linv)
    c_ref[...] = nt(nn(linv, small_ref[3 * w : 4 * w]), linv)


def per_device(prior_basis, cond_x, cond_y, capacitance, pad_mask, port_nodes):
    rows, cols, width = prior_basis.shape
    ngx, ngy = lax.axis_size("gx"), lax.axis_size("gy")
    ext, wide = rows + UP + DOWN, cols + 2 * SIDE
    hbm = pl.BlockSpec(memory_space=pltpu.HBM)
    vmem = pl.BlockSpec(memory_space=pltpu.VMEM)

    def buf(*shape):
        return pltpu.VMEM(shape, F32)

    dma = pltpu.SemaphoreType.DMA
    pcs = (2 * width // ngx, 2 * width // ngx, 6 * width // ngx)
    scratch = [buf(rows, cols)] * 3 + [pltpu.VMEM((rows, cols), jnp.int32), pltpu.VMEM((1, width), jnp.int32)]
    scratch += [buf(width, width), buf(cols, width), buf(3, wide, width), buf(ext, wide, width)]
    scratch += [buf(ext + 1, wide, width), buf(ext, wide + 2 * PAD, width), buf(ext, wide, width)]
    scratch += [buf(ext, wide, width), buf(ext, wide, width)]
    scratch += [buf(ext, wide + 2 * PAD, width), buf(ext, wide + 2 * PAD, width), buf(rows, cols, width)]
    scratch += [buf(pc * ngx, width) for pc in pcs]
    scratch += [buf(ngx, pc, width) for pc in pcs]
    scratch += [buf(pc, width) for pc in pcs]
    scratch += [buf(ngy, pc, width) for pc in pcs]
    scratch += [buf(ngx, pc, width) for pc in pcs]
    scratch += [dma((6,)), dma((8,)), dma((8,)), dma((8,)), dma((8,))] + [dma((3,))] * 6
    field, small = pl.pallas_call(
        functools.partial(reach, ngx, ngy, rows, cols),
        out_shape=(
            jax.ShapeDtypeStruct((rows * cols, width), F32),
            jax.ShapeDtypeStruct((4 * width, width), F32),
        ),
        in_specs=[hbm] * 6,
        out_specs=(vmem, vmem),
        scratch_shapes=scratch,
        compiler_params=pltpu.CompilerParams(
            collective_id=0, has_side_effects=True, vmem_limit_bytes=40 * 1024 * 1024
        ),
    )(prior_basis, cond_x, cond_y, capacitance, pad_mask, port_nodes.reshape(1, width))
    basis, g, c = pl.pallas_call(
        finish,
        out_shape=(
            jax.ShapeDtypeStruct((rows * cols, width), F32),
            jax.ShapeDtypeStruct((width, width), F32),
            jax.ShapeDtypeStruct((width, width), F32),
        ),
        in_specs=[vmem] * 3,
        out_specs=(vmem,) * 3,
        compiler_params=pltpu.CompilerParams(vmem_limit_bytes=16 * 1024 * 1024),
    )(prior_basis.reshape(rows * cols, width), field, small)
    return basis.reshape(rows, cols, width), g, c


def solution(mesh):
    tile = P("gx", "gy")
    return jax.shard_map(
        per_device,
        mesh=mesh,
        in_specs=(P("gx", "gy", None), tile, tile, tile, tile, P()),
        out_specs=(P("gx", "gy", None), P(), P()),
        check_vma=False,
    )
```

time: 934 us -> 74.5 us (0.08)
  waiting for transfers between devices: 817 us -> 0 us
  Pallas kernels: 0 us -> 69.1 us
  starting transfers between devices: 63.1 us -> 0 us
  other arithmetic: 28.1 us -> 0 us
  between operations: 14 us -> 0.65 us
    psum x3 -> x0, waiting for transfers between devices: 789 us -> none  [the longest x1 273 us: per_device(): proj = lax.psum(local_inner(prior_basis, field), ('gx', 'gy')) / nodes]
    pallas_call x0 -> x2, Pallas kernels: none -> 69.1 us  [the longest x1 67.3 us: per_device(): pl.pallas_call(functools.partial(reach, ngx, ngy, rows, cols), out_shape=...]
    ppermute x22 -> x0, starting transfers between devices: 62.9 us -> none  [the longest x10 38.2 us: padded(): lax.ppermute(tail, axis, [(i, (i + 1) % count) for i in range(ends)])]
    ppermute x22 -> x0, waiting for transfers between devices: 28 us -> none  [the longest x10 26.3 us: padded(): lax.ppermute(head, axis, [((i + 1) % count, i) for i in range(ends)])]
    another operation x5 -> x0, other arithmetic: 22.9 us -> none  [the longest x3 12.4 us: per_device(): lower = jnp.linalg.cholesky(gram)]
  transfers between devices with their start and end apart: 25 -> 0, of which waited for: 13 -> 0; matrix products, arithmetic and copies ran while one was open for 0% -> 0% of each run, Pallas kernels for 0% -> 0%
where the time goes in v1:
time: 74.5 us; the launch traced here: 74.2 us
  Pallas kernels  69.1 us (93%)
  local copies, waits for them, and re-layouts  4.38 us (6%)
    pallas_call x1, Pallas kernels, per_device(): pl.pallas_call(functools.partial(reach, ngx, ngy, rows, cols), out_shape=...  67.3 us
    unnamed x12, local copies, waits for them, and re-layouts  4.38 us
    pallas_call x1, Pallas kernels, per_device(): pl.pallas_call(finish, out_shape=(jax.ShapeDtypeStruct((rows * cols, widt...  1.85 us

profile of v1, /device:TPU:1, one launch (start us, length us, event | category | flops | bytes accessed | tf_op | source)
XLA Modules:
  0.0 74.2 jit_solution(8661282538512112796)
XLA Ops:
  0.6 0.0 copy-start.5
  0.6 0.6 copy-done.5
  1.3 0.0 copy-start
  1.3 0.9 %copy-done = f32[16,32,128]{2,1,0:T(8,128)S(1)} copy-done((f32[16,32,128]{2,1,0:T(8,128)S(1)}, f32[16,32,128]{2,1,0:T(8,128)}, u32[]{:S(2)}) %copy-start) | copy-done | bytes 262168
  2.2 0.0 copy-start.1
  2.2 0.7 copy-done.1
  2.9 0.0 copy-start.2
  2.9 0.7 copy-done.2
  3.6 0.0 copy-start.3
  3.6 0.7 copy-done.3
  4.3 0.0 copy-start.4
  4.3 0.7 copy-done.4
  5.0 67.3 %shard_map.85 = (f32[512,128]{1,0:T(8,128)S(1)}, f32[512,128]{1,0:T(8,128)S(1)}) custom-call(f32[16,32,128]{2,1,0:T(8,128)S(1)} %copy-done, f32[16,32]{1,0:T(8,128)S(1)} %copy-done.1, f32[16,32]{1,0:T(8,128)S(1)} %copy-done.2, f32[16,32]{1,0:T(8,128)S(1)} %copy-done.3, s32[16,32]{1,0:T(8,128)S(1)} %copy-done.4, s32[1,128]{1,0:T(1,128)S(1)} %bitcast.4), custom_call_target="tpu_custom_call" | custom-call | tf_op jit(solution)/shard_map/pallas_call | solution.py:384
  72.3 1.8 %shard_map.86 = (f32[512,128]{1,0:T(8,128)}, f32[128,128]{1,0:T(8,128)}, f32[128,128]{1,0:T(8,128)}) custom-call(f32[512,128]{1,0:T(8,128)S(1)} %bitcast.3, f32[512,128]{1,0:T(8,128)S(1)} %get-tuple-element.8.f_ref, f32[512,128]{1,0:T(8,128)S(1)} %get-tuple-element.9.small_ref), custom_call_target="tpu_custom_call" | custom-call | tf_op jit(solution)/shard_map/pallas_call | solution.py:397
Async XLA Ops:
  0.6 0.7 copy-start.5
  1.3 0.9 %copy-start = (f32[16,32,128]{2,1,0:T(8,128)S(1)}, f32[16,32,128]{2,1,0:T(8,128)}, u32[]{:S(2)}) copy-start(f32[16,32,128]{2,1,0:T(8,128)} %v_hbm.1) | copy-start | bytes 786436
  2.2 0.7 copy-start.1
  2.9 0.7 copy-start.2
  3.6 0.7 copy-start.3
  4.3 0.7 copy-start.4

commit v2 on v1

--- a/solution.py
+++ b/solution.py
@@ -49,7 +49,6 @@
     def column(x, k):
         return jnp.broadcast_to(x[:, k : k + 1], x.shape)
 
-    rows = []
     for p in range(n // 8):
         g = tiles[p]
         cols = [column(g, 8 * p + j) for j in range(8)]
@@ -65,7 +64,7 @@
             for l in range(j + 1, 8):
                 cols[l] = jnp.where(here, 0.0, cols[l]) - m * row(cols[l], j)
             g = jnp.where(at, -m, jnp.where(here, 0.0, g) - m * rj)
-        rows.append(jnp.where(lane <= sub + 8 * p, kept, 0.0))
+        yield jnp.where(lane <= sub + 8 * p, kept, 0.0)
         if p + 1 < n // 8:
             w = [row(g, j) for j in range(8)]
             inside = (lane >= 8 * p) & (lane < 8 * p + 8)
@@ -74,7 +73,6 @@
                 for j in range(8):
                     x = x - column(tiles[t], 8 * p + j) * w[j]
                 tiles[t] = x
-    return rows
 
 
 def reach(
@@ -82,8 +80,8 @@
     v_hbm, condx_hbm, condy_hbm, cap_hbm, pad_hbm, port_hbm,
     field_out, small_out,
     t0, t1, t2, t3, port, stack, q, qx, vx, cxs, cys, dis, caps, rhs, fa, fb, dgs,
-    a0, a1, a2, r10, r11, r12, d0, d1, d2, r20, r21, r22, o0, o1, o2,
-    lsem, vsend, vrecv, qsend, qrecv, s1, v1, s2, v2, s3, v3,
+    a0, a1, a2, r10, r11, r12, d0, d1, d2, r20, r21, r22, o0, o1,
+    rc2, h2, hw2, lsem, csend, crecv, vsend, vrecv, qsend, qrecv, s1, v1, s2, v2, s3, v3,
 ):
     gx, gy = lax.axis_index("gx"), lax.axis_index("gy")
     width = 128
@@ -91,6 +89,25 @@
     wide = cols + 2 * SIDE
     nx, ny = ngx * rows, ngy * cols
     nodes = nx * ny
+
+    barrier = pltpu.get_barrier_semaphore()
+    around = [(dx, dy) for dx in (-1, 0, 1) for dy in (-1, 0, 1) if dx or dy]
+
+    def beside(dx, dy):
+        return lax.rem(gx + ngx + dx, ngx), lax.rem(gy + ngy + dy, ngy)
+
+    for dx, dy in around:
+        pl.semaphore_signal(barrier, inc=1, device_id=beside(dx, dy), device_id_type=MESH)
+
+    def others(me, n, f, lo=1):
+        def step(k, c):
+            f(lax.rem(me + k, n))
+            return c
+
+        lax.fori_loop(lo, n + 1 - lo, step, 0)
+
+    others(gx, ngx, lambda p: pl.semaphore_signal(barrier, inc=1, device_id=(p, gy), device_id_type=MESH), 2)
+    others(gy, ngy, lambda p: pl.semaphore_signal(barrier, inc=1, device_id=(gx, p), device_id_type=MESH), 2)
 
     loads = [
         pltpu.make_async_copy(s, d, lsem.at[k])
@@ -101,26 +118,6 @@
     ]
     for copy in loads:
         copy.start()
-
-    barrier = pltpu.get_barrier_semaphore()
-    around = [(dx, dy) for dx in (-1, 0, 1) for dy in (-1, 0, 1) if dx or dy]
-
-    def beside(dx, dy):
-        return lax.rem(gx + ngx + dx, ngx), lax.rem(gy + ngy + dy, ngy)
-
-    for dx, dy in around:
-        if dx and dy:
-            pl.semaphore_signal(barrier, inc=1, device_id=beside(dx, dy), device_id_type=MESH)
-
-    def others(me, n, f):
-        def step(k, c):
-            f(lax.rem(me + k, n))
-            return c
-
-        lax.fori_loop(1, n, step, 0)
-
-    others(gx, ngx, lambda p: pl.semaphore_signal(barrier, inc=1, device_id=(p, gy), device_id_type=MESH))
-    others(gy, ngy, lambda p: pl.semaphore_signal(barrier, inc=1, device_id=(gx, p), device_id_type=MESH))
 
     stack[...] = jnp.zeros_like(stack)
     for copy in loads[:5]:
@@ -174,16 +171,20 @@
         return x
 
     def exchange(part, landed, send, recv):
+        slots = landed.shape[0]
+        step = ngy // slots
+        me = gy // step
+
         def one(p):
             pltpu.make_async_remote_copy(
-                part, landed.at[gy], send, recv, device_id=(gx, p), device_id_type=MESH
+                part, landed.at[me], send, recv,
+                device_id=(gx, p * step + lax.rem(gy, step)), device_id_type=MESH,
             ).start()
 
-        others(gy, ngy, one)
-        landed[gy] = part[...]
+        others(me, slots, one)
+        landed[me] = part[...]
 
     def gather(value, whole, send, recv):
-        pc = whole.shape[1]
         whole[gx] = value
 
         def one(p):
@@ -193,7 +194,18 @@
 
         others(gx, ngx, one)
 
-    sets = ((a0, r10, d0, r20, o0), (a1, r11, d1, r21, o1), (a2, r12, d2, r22, o2))
+    core = lax.rem(gy, 2)
+    mate = (gx, gy + 1 - 2 * core)
+    half = 2 * width
+    to_mate = pltpu.make_async_remote_copy(
+        a2.at[pl.ds(pl.multiple_of((1 - core) * half, 8), half)], rc2, csend.at[0], crecv.at[0],
+        device_id=mate, device_id_type=MESH,
+    )
+    back = pltpu.make_async_remote_copy(
+        hw2.at[core], hw2.at[core], csend.at[1], crecv.at[1], device_id=mate, device_id_type=MESH
+    )
+
+    sets = ((a0, r10, d0, r20, o0), (a1, r11, d1, r21, o1), (h2, r12, d2, r22, hw2.at[core]))
 
     def first(k):
         scatter(sets[k][0], sets[k][1], s1.at[k], v1.at[k])
@@ -204,19 +216,17 @@
         exchange(sets[k][2], sets[k][3], s2.at[k], v2.at[k])
 
     def third(k):
-        wait(sets[k][3], ngy, v2.at[k])
+        wait(sets[k][3], sets[k][3].shape[0], v2.at[k])
         gather(total(sets[k][3]), sets[k][4], s3.at[k], v3.at[k])
 
     def last(k):
         wait(sets[k][4], ngx, v3.at[k])
 
     def block(k, b):
-        whole = sets[k][4]
-        pc = whole.shape[1]
-        per = width // pc if pc <= width else 0
-        if per and width % pc == 0:
-            return whole[b * per : (b + 1) * per].reshape(width, width)
-        return whole[...].reshape(-1, width)[b * width : (b + 1) * width]
+        return sets[k][4][...].reshape(2 * width, width)[b * width : (b + 1) * width]
+
+    wr = lax.broadcasted_iota(jnp.int32, (width, width), 0)
+    wc = lax.broadcasted_iota(jnp.int32, (width, width), 1)
 
     qx[1, SIDE : SIDE + cols] = q[...]
     loads[5].wait()
@@ -292,15 +302,12 @@
 
         lax.fori_loop(1 + s, ext - 1 - s, sweep, 0)
         src, dst = dst, src
-        if s == 1:
-            second(0)
 
     own_f = slice(PAD + SIDE, PAD + SIDE + cols)
     f = src[own_r, own_f].reshape(rows * cols, width)
     a1[0:width] = tn(v, f)
     a1[width : 2 * width] = tn(f, f)
     first(1)
-    third(0)
     field_out[...] = f
 
     cxo = cxs[UP + 1 : UP + 1 + rows, own_c].reshape(rows * cols, width)
@@ -313,39 +320,56 @@
     uv = cxo * v_below + cyo * v_right
     uf = cxo * f_below + cyo * f_right
     gv = dgo * v - uv
-    a2[0:width] = tn(v, gv) - tn(uv, v)
-    a2[width : 2 * width] = tn(gv, f) - tn(v, uf)
-    a2[2 * width : 3 * width] = tn(f, dgo * f - uf) - tn(uf, f)
+    vgv = tn(v, gv) - tn(uv, v)
+    fgf = tn(f, dgo * f - uf) - tn(uf, f)
     cf = c_own * f
+    fcf = tn(f, cf)
+    corner = jnp.sum(jnp.where(wr == wc, fcf, 0.0), axis=0, keepdims=True)
+    spare = jnp.where(wr == 0, corner, jnp.where(wc == width - 1, pltpu.roll(corner, width - 1, 1), 0.0))
+    a2[0:width] = jnp.where(wr >= wc, vgv, spare)
+    a2[width : 2 * width] = jnp.where(wr >= wc, fgf, fcf)
+    a2[2 * width : 3 * width] = tn(gv, f) - tn(v, uf)
     a2[3 * width : 4 * width] = tn(v, cf)
-    a2[4 * width : 5 * width] = tn(f, cf)
-    a2[5 * width :] = jnp.zeros((a2.shape[0] - 5 * width, width), F32)
+    to_mate.start()
+    second(0)
+    to_mate.wait_recv()
+    h2[...] = a2[pl.ds(pl.multiple_of(core * half, 8), half)] + rc2[...]
+    first(2)
     second(1)
-    first(2)
+    third(0)
+    second(2)
     third(1)
-    second(2)
     last(0)
+    third(2)
     last(1)
-
     vv, vcv = block(0, 0) / nodes, block(0, 1) / nodes
     proj, ff = block(1, 0) / nodes, block(1, 1) / nodes
     z = nn(vv, proj) - 2.0 * proj
     gram = ff + tn(proj, z)
-    third(2)
     for t, r in enumerate(inverse_factor(gram)):
         small_out[8 * t : 8 * t + 8] = r
+        if t == 10:
+            last(2)
+            back.start()
     small_out[width : 2 * width] = proj
-    last(2)
-    vgv, vgf, fgf = (block(2, b) / nodes for b in range(3))
-    vcf, fcf = (block(2, b) / nodes for b in range(3, 5))
+    back.wait_recv()
+    sums = hw2[...].reshape(4, width, width) / nodes
+
+    def both(tri, keep):
+        return jnp.where(keep, tri, 0.0) + jnp.where(wr == wc, 0.0, jnp.where(keep, tri, 0.0)).T
+
+    vgf, vcf = sums[2], sums[3]
+    vgv, fgf = both(sums[0], wr >= wc), both(sums[1], wr >= wc)
+    corner = jnp.where(wc[0:1] == 0, pltpu.roll(sums[0, 1:2], 1, 1), sums[0, 0:1])
+    fcf = both(sums[1], wr < wc) + jnp.where(wr == wc, corner, 0.0)
     small_out[2 * width : 3 * width] = fgf - tn(vgf, proj) + tn(proj, nn(vgv, proj) - vgf)
     small_out[3 * width : 4 * width] = fcf - tn(vcf, proj) + tn(proj, nn(vcv, proj) - vcf)
 
-    for copy in sent:
+    for copy in sent + [to_mate, back]:
         copy.wait_send()
     for k in range(3):
         wait(sets[k][1], ngx, s1.at[k])
-        wait(sets[k][3], ngy, s2.at[k])
+        wait(sets[k][3], sets[k][3].shape[0], s2.at[k])
         wait(sets[k][4], ngx, s3.at[k])
 
 
@@ -369,18 +393,18 @@
         return pltpu.VMEM(shape, F32)
 
     dma = pltpu.SemaphoreType.DMA
-    pcs = (2 * width // ngx, 2 * width // ngx, 6 * width // ngx)
+    pc = 2 * width // ngx
     scratch = [buf(rows, cols)] * 3 + [pltpu.VMEM((rows, cols), jnp.int32), pltpu.VMEM((1, width), jnp.int32)]
     scratch += [buf(width, width), buf(cols, width), buf(3, wide, width), buf(ext, wide, width)]
     scratch += [buf(ext + 1, wide, width), buf(ext, wide + 2 * PAD, width), buf(ext, wide, width)]
     scratch += [buf(ext, wide, width), buf(ext, wide, width)]
     scratch += [buf(ext, wide + 2 * PAD, width), buf(ext, wide + 2 * PAD, width), buf(rows, cols, width)]
-    scratch += [buf(pc * ngx, width) for pc in pcs]
-    scratch += [buf(ngx, pc, width) for pc in pcs]
-    scratch += [buf(pc, width) for pc in pcs]
-    scratch += [buf(ngy, pc, width) for pc in pcs]
-    scratch += [buf(ngx, pc, width) for pc in pcs]
-    scratch += [dma((6,)), dma((8,)), dma((8,)), dma((8,)), dma((8,))] + [dma((3,))] * 6
+    scratch += [buf(2 * width, width), buf(2 * width, width), buf(4 * width, width)]
+    scratch += [buf(ngx, pc, width)] * 3 + [buf(pc, width)] * 3
+    scratch += [buf(ngy, pc, width), buf(ngy, pc, width), buf(ngy // 2, pc, width)]
+    scratch += [buf(ngx, pc, width)] * 2
+    scratch += [buf(2 * width, width), buf(2 * width, width), buf(2, ngx, 2 * width // ngx, width)]
+    scratch += [dma((6,)), dma((2,)), dma((2,)), dma((8,)), dma((8,)), dma((8,)), dma((8,))] + [dma((3,))] * 6
     field, small = pl.pallas_call(
         functools.partial(reach, ngx, ngy, rows, cols),
         out_shape=(
@@ -391,7 +415,7 @@
         out_specs=(vmem, vmem),
         scratch_shapes=scratch,
         compiler_params=pltpu.CompilerParams(
-            collective_id=0, has_side_effects=True, vmem_limit_bytes=40 * 1024 * 1024
+            collective_id=0, has_side_effects=True, vmem_limit_bytes=60 * 1024 * 1024
         ),
     )(prior_basis, cond_x, cond_y, capacitance, pad_mask, port_nodes.reshape(1, width))
     basis, g, c = pl.pallas_call(
@@ -403,7 +427,7 @@
         ),
         in_specs=[vmem] * 3,
         out_specs=(vmem,) * 3,
-        compiler_params=pltpu.CompilerParams(vmem_limit_bytes=16 * 1024 * 1024),
+        compiler_params=pltpu.CompilerParams(vmem_limit_bytes=60 * 1024 * 1024),
     )(prior_basis.reshape(rows * cols, width), field, small)
     return basis.reshape(rows, cols, width), g, c
 

time: 74.5 us -> 58.1 us (0.78)
  Pallas kernels: 69.1 us -> 57.3 us
  local copies, waits for them, and re-layouts: 4.38 us -> 0 us
    pallas_call x1, Pallas kernels: 67.3 us -> 54.3 us  [per_device(): pl.pallas_call(functools.partial(reach, ngx, ngy, rows, cols), out_shape=...]
    unnamed x12 -> x0, local copies, waits for them, and re-layouts: 4.38 us -> none
    pallas_call x1, Pallas kernels: 1.85 us -> 2.95 us  [per_device(): pl.pallas_call(finish, out_shape=(jax.ShapeDtypeStruct((rows * cols, widt...]
where the time goes in v2:
time: 58.1 us; the launch traced here: 57.9 us
  Pallas kernels  57.3 us (99%)
  between operations  0.64 us (1%)
    pallas_call x1, Pallas kernels, per_device(): pl.pallas_call(functools.partial(reach, ngx, ngy, rows, cols), out_shape=...  54.3 us
    pallas_call x1, Pallas kernels, per_device(): pl.pallas_call(finish, out_shape=(jax.ShapeDtypeStruct((rows * cols, widt...  2.95 us

profile of v2, /device:TPU:1, one launch (start us, length us, event | category | flops | bytes accessed | tf_op | source)
XLA Modules:
  0.0 57.9 jit_solution(10919355531105673870)
XLA Ops:
  0.6 54.3 %shard_map.85 = (f32[512,128]{1,0:T(8,128)}, f32[512,128]{1,0:T(8,128)}) custom-call(f32[16,32,128]{2,1,0:T(8,128)} %v_hbm.1, f32[16,32]{1,0:T(8,128)} %condx_hbm.1, f32[16,32]{1,0:T(8,128)} %condy_hbm.1, f32[16,32]{1,0:T(8,128)} %cap_hbm.1, s32[16,32]{1,0:T(8,128)} %pad_hbm.1, s32[1,128]{1,0:T(1,128)} %bitcast.4), custom_call_target="tpu_custom_call" | custom-call | tf_op jit(solution)/shard_map/pallas_call | solution.py:408
  55.0 3.0 %shard_map.86 = (f32[512,128]{1,0:T(8,128)}, f32[128,128]{1,0:T(8,128)}, f32[128,128]{1,0:T(8,128)}) custom-call(f32[512,128]{1,0:T(8,128)} %bitcast.3, f32[512,128]{1,0:T(8,128)} %get-tuple-element.8.f_ref, f32[512,128]{1,0:T(8,128)} %get-tuple-element.9.small_ref), custom_call_target="tpu_custom_call" | custom-call | tf_op jit(solution)/shard_map/pallas_call | solution.py:421
